TPU v7x, 512 devices: a whole 4x4x16 slice. The times are simulated.
512 devices in a mesh: pipe: 2 (over core), dp: 16 (over y, x), tensor: 16 (over z).
Axes of the slice: x: 4, y: 4, z: 16, core: 2. Of those that a mesh axis runs over, the one named last changes fastest.
Arguments:
- x_act: bfloat16 [2, 6144, 16384], P('pipe', 'dp', 'tensor'), may hold values from -6 to 6
- grad_z: bfloat16 [2, 6144, 26624], P('pipe', 'dp', 'tensor'), may hold values from -6 to 6
- weight_tiles: bfloat16 [2, 256, 128, 128], P('pipe', 'tensor'), may hold values from -0.5 to 0.5
- tile_rows: int32 [2, 256], P('pipe', 'tensor'), may hold values from 0 to 127, as said below
- tile_cols: int32 [2, 256], P('pipe', 'tensor'), may hold values from 0 to 12
- err_in: float32 [2, 16, 256, 128, 128], P('pipe', 'dp', 'tensor'), may hold values from -0.3 to 0.3
- kept_mask: int32 [2, 16, 256], P('pipe', 'dp', 'tensor'), may hold values 0 or 1
- tile_list: int32 [2, 16, 192], P('pipe', 'dp', 'tensor'), may hold values from 0 to 23, as said below
- live_count: int32 [2, 16, 16], P('pipe', 'dp', 'tensor'), may hold values from 1 to 12, as said below
Outputs:
- recv_tiles: bfloat16 [2, 16, 192, 128, 128], P('pipe', 'dp', 'tensor')
- err_out: float32 [2, 16, 256, 128, 128], P('pipe', 'dp', 'tensor')
- grad_sum: float32 [2, 16, 16, 128, 128], P('pipe', 'dp', 'tensor')
Inputs may be any that keep to these rules, and one draw needn't show every extreme that they name: `tile_rows`: entry j of a tensor rank's 16 entries of one section names a column block held by tensor rank j // (16 / 16), that is one of the blocks ((j // (16 / 16)) * L to that plus L - 1, L = 16384 / (128 * 16)). `tile_list`: A device's 12 entries are distinct tile numbers m * L + b of its own region (L = 16384 / (128 * 16), m < 3, b < L). `live_count`: some device uses all 12 entries of its list.
All inputs are finite; a program needn't handle non-finite values. No bound on the sum of `kept_mask` on one device may be relied on, other than what follows from the above.
Results may differ from a plain program's by a relative error of at most 0.0048.
Values may be sent and summed in bfloat16 or wider, within the bound.
A program may use at most 128 MiB of HBM per device.

v0:
```python
import jax
import jax.numpy as jnp
from jax import lax
from jax.sharding import PartitionSpec as P


def shifted(value, axis, by):
    count = lax.axis_size(axis)
    return lax.ppermute(value, axis, [(i, (i + by) % count) for i in range(count)])


def pack_listed(input_grad, listed, live_now, tile_size, local_blocks):
    tok_count = input_grad.shape[0]
    grid = input_grad.reshape(tok_count // tile_size, tile_size, local_blocks, tile_size)
    picked = grid[listed // local_blocks, :, listed % local_blocks, :]
    valid = jnp.arange(listed.shape[0], dtype=jnp.int32) < live_now[0]
    return jnp.where(valid[:, None, None], picked, jnp.zeros_like(picked))


def local(
    x_act, grad_z, weight_tiles, tile_rows, tile_cols, err_in, kept_mask, tile_list, live_count
):
    tensor_count = lax.axis_size("tensor")
    inputs = x_act[0]
    grads_out = grad_z[0]
    stored = weight_tiles[0]
    row_ids = tile_rows[0]
    col_ids = tile_cols[0]
    tok_count = inputs.shape[0]
    tile_size = stored.shape[1]
    local_blocks = inputs.shape[1] // tile_size
    local_rows = row_ids % local_blocks
    grad_blocks = grads_out.reshape(tok_count, grads_out.shape[1] // tile_size, tile_size)
    grad_sel = jnp.take(grad_blocks, col_ids, axis=1)
    gathered = lax.all_gather(inputs, "tensor", axis=1, tiled=True)
    input_sel = jnp.take(
        gathered.reshape(tok_count, local_blocks * tensor_count, tile_size), row_ids, axis=1
    )
    weight_grads = jnp.einsum(
        "tkc,tkf->kcf", input_sel, grad_sel, preferred_element_type=jnp.float32
    ) * (1.0 / tok_count)
    accumulated = weight_grads + err_in[0, 0]
    keep_now = (kept_mask[0, 0] == 1)[:, None, None]
    sent_tiles = jnp.where(keep_now, accumulated, jnp.float32(0.0))
    residual = accumulated - sent_tiles
    summed = lax.psum_scatter(sent_tiles, "dp", scatter_dimension=0, tiled=True)
    partial_value = jnp.einsum(
        "tkf,kcf->tkc", grad_sel, stored, preferred_element_type=jnp.float32
    ).astype(jnp.bfloat16)
    arrived_terms, arrived_rows = (
        lax.all_to_all(partial_value, "tensor", split_axis=1, concat_axis=1, tiled=True),
        lax.all_to_all(local_rows[None, :], "tensor", split_axis=1, concat_axis=1, tiled=True),
    )
    onehot = (
        arrived_rows[0][:, None] == jnp.arange(local_blocks, dtype=jnp.int32)[None, :]
    ).astype(jnp.bfloat16)
    input_grad = jnp.einsum(
        "trc,rb->tbc", arrived_terms, onehot, preferred_element_type=jnp.float32
    ).astype(jnp.bfloat16)
    listed = tile_list[0, 0]
    live_now = live_count[0, 0]
    grad_in, listed_in, live_in = shifted((input_grad, listed, live_now), "pipe", -1)
    arrived = pack_listed(grad_in, listed_in, live_in, tile_size, local_blocks)
    return (arrived[None, None], residual[None, None], summed[None, None])


def solution(mesh):
    return jax.shard_map(
        local,
        mesh=mesh,
        in_specs=(
            P("pipe", "dp", "tensor"),
            P("pipe", "dp", "tensor"),
            P("pipe", "tensor", None, None),
            P("pipe", "tensor"),
            P("pipe", "tensor"),
            P("pipe", "dp", "tensor", None, None),
            P("pipe", "dp", "tensor"),
            P("pipe", "dp", "tensor"),
            P("pipe", "dp", "tensor"),
        ),
        out_specs=(
            P("pipe", "dp", "tensor", None, None),
            P("pipe", "dp", "tensor", None, None),
            P("pipe", "dp", "tensor", None, None),
        ),
        check_vma=False,
    )
```

profile of v0, /device:TPU:32, one launch (start us, length us, event | category | flops | bytes accessed | tf_op | source)
XLA Modules:
  0.0 350.0 jit_solution(13440303011730557698)
XLA Ops:
  7.2 0.0 copy-start
  7.2 0.0 copy-start.5
  7.2 0.0 copy-start.2
  7.2 0.0 all-gather.3.cloned.1.call-start
  7.2 2.4 copy.37
  9.7 0.0 all-gather.3.cloned.1.call-update
  9.7 0.0 copy-done.5
  9.7 0.7 copy.32
  10.4 15.2 %all-to-all-start = ((s32[1,16,1]{2,0,1:T(1,128)}), s32[1,16,1]{2,0,1:T(1,128)S(1)}, u32[]{:S(2)}, u32[]{:S(2)}) async-start(s32[1,16,1]{2,0,1:T(1,128)} %copy.32), calls=%async_computation | async-start | bytes 16384 | tf_op jit(solution)/shard_map/all_to_all | solution.py:52
  25.6 0.0 copy-done.2
  25.6 1.7 copy.33
  27.3 0.0 copy-start.4
  27.3 2.1 copy.34
  29.4 0.0 copy-done.4
  29.4 0.9 gather_fusion
  30.3 0.0 copy-start.1
  30.3 0.0 copy-done
  30.3 1.8 fusion.8
  32.1 0.0 copy-done.1
  32.1 0.0 copy-start.6
  32.1 4.6 %all-to-all-done = s32[1,16,1]{2,0,1:T(1,128)S(1)} async-done(((s32[1,16,1]{2,0,1:T(1,128)}), s32[1,16,1]{2,0,1:T(1,128)S(1)}, u32[]{:S(2)}, u32[]{:S(2)}) %all-to-all-start) | async-done | bytes 96 | tf_op jit(solution)/shard_map/all_to_all | solution.py:52
  36.8 7.6 %all-to-all-start.1 = ((bf16[384,16,128]{2,0,1:T(8,128)(2,1)}), bf16[384,16,128]{2,0,1:T(8,128)(2,1)S(1)}, u32[]{:S(2)}, u32[]{:S(2)}) async-start(bf16[384,16,128]{2,0,1:T(8,128)(2,1)} %fusion.8), calls=%async_computation.1 | async-start | bytes 3145728 | tf_op jit(solution)/shard_map/all_to_all | solution.py:51
  44.3 0.0 reduce-scatter.4.cloned.1.call-start
  44.4 0.0 copy-done.6
  44.4 183.4 %all-gather.3.cloned.1.call-done = bf16[1,384,16384]{1,2,0:T(8,128)(2,1)} async-done(((bf16[1,384,1024]{1,2,0:T(8,128)(2,1)}), bf16[1,384,16384]{1,2,0:T(8,128)(2,1)}) %all-gather.3.cloned.1.call-update) | async-done | bytes 12582928 | tf_op jit(solution)/shard_map/all_gather | solution.py:35
  227.9 15.8 %copy.38 = bf16[384,128,128]{2,0,1:T(8,128)(2,1)} copy(bf16[384,128,128]{0,2,1:T(8,128)(2,1)} %bitcast.64) | data formatting | bytes 25165824 | tf_op jit(solution)/shard_map/reshape | solution.py:37
  243.7 0.0 copy-start.3
  243.7 6.6 %gather_fusion.2 = bf16[16,384,128]{2,1,0:T(8,128)(2,1)} fusion(bf16[384,128,128]{2,0,1:T(8,128)(2,1)} %copy.38, s32[1024]{0:T(1024)S(1)} %pad_clamp_fusion), kind=kCustom, calls=%fused_computation.2 | custom fusion | bytes 3145792 | tf_op jit(solution)/shard_map/jit(_take)/gather | solution.py:36
  250.3 0.0 copy-done.3
  250.3 4.1 %broadcast_select_fusion.3 = (f32[16,128,128]{2,1,0:T(8,128)}, f32[1,1,16,128,128]{4,3,2,1,0:T(8,128)}) fusion(pred[16]{0:T(512)(128)(4,1)S(1)} %compare_bitcast_fusion, f32[1,1,16,128,128]{4,3,2,1,0:T(8,128)S(1)} %copy-done.3, bf16[16,384,128]{2,1,0:T(8,128)(2,1)} %copy-done.1, pred[16]{0:T(512)(128)(4,1)S(1)} %compare_and_fusion.1, ...), kind=kOutput, calls=%fused_computation.21 | convolution fusion | flops 203948032 | bytes 6291504 | tf_op jit(solution)/shard_map/tkc,tkf->kcf/dot_general | solution.py:39
  254.4 0.0 copy-start.7
  254.4 0.0 reduce-scatter.4.cloned.1.call-update
  254.4 0.4 reduce
  254.8 0.0 all-to-all-done.1
  254.8 0.9 fusion.24
  255.7 1.9 collective-permute-start.1
  257.7 0.0 copy-done.7
  257.7 2.4 collective-permute-start.2
  260.1 1.9 collective-permute-start
  262.0 1.4 collective-permute-done
  263.4 0.6 iota_compare_fusion.1
  264.0 0.0 collective-permute-done.2
  264.1 0.0 collective-permute-done.1
  264.1 0.2 copy.36
  264.2 0.7 gather_fusion.1
  264.9 0.8 bitcast_select_fusion
  265.8 77.4 %reduce-scatter.4.cloned.1.call-done = f32[1,128,128]{2,1,0:T(8,128)} async-done(((f32[16,128,128]{2,1,0:T(8,128)}), f32[1,128,128]{2,1,0:T(8,128)}) %reduce-scatter.4.cloned.1.call-update) | async-done | bytes 65552
  (9 shorter events, 0.1 us)
Async XLA Ops:
  7.2 23.1 %copy-start = (bf16[1,16,128,128]{3,2,1,0:T(8,128)(2,1)S(1)}, bf16[1,16,128,128]{3,2,1,0:T(8,128)(2,1)}, u32[]{:S(2)}) copy-start(bf16[1,16,128,128]{3,2,1,0:T(8,128)(2,1)} %param.11) | copy-start | bytes 1572868
  7.2 2.5 copy-start.5
  7.2 18.4 %copy-start.2 = (bf16[1,384,1664]{2,1,0:T(8,128)(2,1)S(1)}, bf16[1,384,1664]{2,1,0:T(8,128)(2,1)}, u32[]{:S(2)}) copy-start(bf16[1,384,1664]{2,1,0:T(8,128)(2,1)} %param.10) | copy-start | bytes 3833860
  7.2 220.7 %all-gather.3.cloned.1.call-start = ((), (), s32[]{:S(2)}) async-start(), calls=%async_computation.3 | async-start | bytes 13369344 | tf_op jit(solution)/shard_map/all_gather | solution.py:35
  10.4 26.4 %all-to-all-start = ((s32[1,16,1]{2,0,1:T(1,128)}), s32[1,16,1]{2,0,1:T(1,128)S(1)}, u32[]{:S(2)}, u32[]{:S(2)}) async-start(s32[1,16,1]{2,0,1:T(1,128)} %copy.32), calls=%async_computation | async-start | bytes 16384 | tf_op jit(solution)/shard_map/all_to_all | solution.py:52
  27.3 2.1 copy-start.4
  30.3 1.9 copy-start.1
  32.1 12.3 %copy-start.6 = (s32[1,1,16]{2,1,0:T(1,128)S(1)}, s32[1,1,16]{2,1,0:T(1,128)}, u32[]{:S(2)}) copy-start(s32[1,1,16]{2,1,0:T(1,128)} %param.15) | copy-start | bytes 196
  36.8 218.0 %all-to-all-start.1 = ((bf16[384,16,128]{2,0,1:T(8,128)(2,1)}), bf16[384,16,128]{2,0,1:T(8,128)(2,1)S(1)}, u32[]{:S(2)}, u32[]{:S(2)}) async-start(bf16[384,16,128]{2,0,1:T(8,128)(2,1)} %fusion.8), calls=%async_computation.1 | async-start | bytes 3145728 | tf_op jit(solution)/shard_map/all_to_all | solution.py:51
  44.3 298.8 %reduce-scatter.4.cloned.1.call-start = ((), (), s32[]{:S(2)}) async-start(), calls=%async_computation.4 | async-start | bytes 1114112
  243.7 6.6 %copy-start.3 = (f32[1,1,16,128,128]{4,3,2,1,0:T(8,128)S(1)}, f32[1,1,16,128,128]{4,3,2,1,0:T(8,128)}, u32[]{:S(2)}) copy-start(f32[1,1,16,128,128]{4,3,2,1,0:T(8,128)} %param.14) | copy-start | bytes 3145732
  254.4 3.3 copy-start.7
  255.7 8.3 %collective-permute-start.1 = (bf16[384,8,128]{2,1,0:T(8,128)(2,1)S(1)}, bf16[384,8,128]{2,1,0:T(8,128)(2,1)S(1)}, u32[]{:S(2)}, u32[]{:S(2)}) collective-permute-start(bf16[384,8,128]{2,1,0:T(8,128)(2,1)S(1)} %fusion.24), channel_id=1, source_target_pairs={{0,256},{256,0},{1,257},{257,1},{2,258},{258,2},{3,259},{259,3},{4... | collective-permute-start | bytes 2359304 | tf_op jit(solution)/shard_map/ppermute | solution.py:9
  257.7 6.3 %collective-permute-start.2 = (s32[12]{0:T(128)S(1)}, s32[12]{0:T(128)S(1)}, u32[]{:S(2)}, u32[]{:S(2)}) collective-permute-start(s32[12]{0:T(128)S(1)} %bitcast.68), channel_id=1, source_target_pairs={{0,256},{256,0},{1,257},{257,1},{2,258},{258,2},{3,259},{259,3},{4... | collective-permute-start | bytes 152 | tf_op jit(solution)/shard_map/ppermute | solution.py:9
  260.1 3.3 collective-permute-start
Sparse Core Ops, SparseCore 0:
  10.7 217.1 all-gather.2
  254.5 88.5 reduce-scatter.3
where the time goes:
time: 351 us; the launch traced here: 350 us
  waiting for transfers between devices  267 us (76%)
  local copies, waits for them, and re-layouts  31 us (9%)
  starting transfers between devices  29.1 us (8%)
  between operations  14.3 us (4%)
  matrix products  6.86 us (2%)
    all_gather x1, waiting for transfers between devices, local(): gathered = lax.all_gather(inputs, 'tensor', axis=1, tiled=True)  183 us
    unnamed x3, waiting for transfers between devices  77.4 us
    reshape x1, local copies, waits for them, and re-layouts, local(): gathered.reshape(tok_count, local_blocks * tensor_count, tile_size)  15.8 us
    all_to_all x1, starting transfers between devices, local(): lax.all_to_all(local_rows[None, :], 'tensor', split_axis=1, concat_axis=1...  15.2 us
    all_to_all x1, starting transfers between devices, local(): lax.all_to_all(partial_value, 'tensor', split_axis=1, concat_axis=1, tile...  7.55 us
  transfers between devices with their start and end apart: 7, of which 4 were waited for; matrix products, arithmetic and copies ran while one was open for 11% of the time, Pallas kernels for 0%

commit v1 on v0

v1 whole, which is shorter than its diff:
```python
import functools

import jax
import jax.numpy as jnp
from jax import lax
from jax.experimental import pallas as pl
from jax.experimental.pallas import tpu as pltpu
from jax.sharding import PartitionSpec as P

MESH = pl.DeviceIdType.MESH
WINDOW = 4
LAG = 2
BF16, F32 = jnp.bfloat16, jnp.float32


def kernel(
    n, n_dp, x_hbm, z_hbm, w_hbm, err_hbm, rows_s, cols_s, mask_s, list_s, live_s,
    recv_o, err_o, sum_o,
    xv, zv, errv, zsend, zrecv, wz, wfull, idx_out, idx_in, idx_s, gsend, grecv, eout, sbuf, sumr, sumv, part, acc, packed,
    zl_sem, xl_sem, load_sem, ix_s, ix_r, ws_s, ws_r, wb_s, wb_r, zs_s, zs_r, gr_s, gr_r, dp_s, dp_r, pp_s, pp_r, eo_s, misc,
):
    tok, blk = zsend.shape[1], zsend.shape[2]
    rounds = n - 1
    local_blocks, hidden_blocks = xv.shape[0], zv.shape[0]
    slots = acc.shape[0]
    chunks, chunk_rows = wfull.shape[2], wfull.shape[3]
    p, d, t = lax.axis_index("pipe"), lax.axis_index("dp"), lax.axis_index("tensor")
    part_of, half = lax.rem(d, chunks), lax.div(d, chunks)
    halves = n_dp // chunks

    def offset(k):
        q = k + 1
        dist = n // 2 - lax.div(q, 2)
        return dist + (1 - lax.rem(q, 2)) * (n - 2 * dist)

    def to_of(k):
        return lax.rem(t + offset(k), n)

    def from_of(k):
        return lax.rem(t + n - offset(k), n)

    def remote(src, dst, s_sem, r_sem, where):
        return pltpu.make_async_remote_copy(
            src_ref=src, dst_ref=dst, send_sem=s_sem, recv_sem=r_sem, device_id=where, device_id_type=MESH
        )

    def z_copy(k):
        return remote(zsend.at[k], zrecv.at[k], zs_s.at[k], zs_r.at[k], {"tensor": to_of(k)})

    def idx_copy(k):
        return remote(idx_out, idx_in.at[k], ix_s.at[k], ix_r.at[k], {"tensor": to_of(k)})

    def w_copy(k):
        src = w_hbm.at[0, to_of(k), pl.ds(pl.multiple_of(part_of * chunk_rows, chunk_rows), chunk_rows)]
        return remote(src, wz.at[lax.div(t, halves), lax.rem(t, halves)], ws_s.at[k], ws_r.at[k], {"tensor": to_of(k)})

    def w_share(i):
        return remote(
            wz.at[:, half], wfull.at[:, half, part_of], wb_s.at[i], wb_r.at[i], {"dp": lax.rem(d + i + 1, n_dp)}
        )

    def g_copy(k):
        return remote(gsend.at[k], grecv.at[k], gr_s.at[k], gr_r.at[k], {"tensor": from_of(k)})

    z_loads = [
        pltpu.make_async_copy(z_hbm.at[0, :, pl.ds(i * blk, blk)], zv.at[i], zl_sem.at[i])
        for i in range(hidden_blocks)
    ]
    x_loads = [
        pltpu.make_async_copy(x_hbm.at[0, :, pl.ds(i * blk, blk)], xv.at[i], xl_sem.at[i])
        for i in range(local_blocks)
    ]
    err_load = pltpu.make_async_copy(err_hbm.at[0, 0], errv, load_sem.at[0])
    for load in (*z_loads, *x_loads, err_load):
        load.start()
    own_w = pltpu.make_async_copy(
        w_hbm.at[0, t, pl.ds(pl.multiple_of(part_of * chunk_rows, chunk_rows), chunk_rows)],
        wz.at[lax.div(t, halves), lax.rem(t, halves)],
        load_sem.at[1],
    )
    own_w.start()

    barrier = pltpu.get_barrier_semaphore()

    def greet_z(i, carry):
        pl.semaphore_signal(barrier, inc=1, device_id={"tensor": lax.rem(t + i, n)}, device_id_type=MESH)
        return carry

    def greet_dp(i, carry):
        pl.semaphore_signal(barrier, inc=1, device_id={"dp": lax.rem(d + i, n_dp)}, device_id_type=MESH)
        return carry

    lax.fori_loop(1, n, greet_z, 0)
    lax.fori_loop(1, n_dp, greet_dp, 0)
    pl.semaphore_signal(barrier, inc=1, device_id={"pipe": 1 - p}, device_id_type=MESH)

    lane = lax.broadcasted_iota(jnp.int32, idx_out.shape, 1)
    row = jnp.zeros(idx_out.shape, jnp.int32)
    for j in range(n):
        row = jnp.where(lane == j, rows_s[0, j], row)
    idx_out[...] = row

    def z_block(j):
        return zv[cols_s[0, j]]

    for load in z_loads:
        load.wait()

    def pick(k, carry):
        zsend[k] = z_block(to_of(k))
        return carry

    lax.fori_loop(0, rounds, pick, 0)

    pl.semaphore_wait(barrier, n - 1 + n_dp - 1 + 1)

    def small(k, carry):
        idx_copy(k).start()
        w_copy(k).start()
        return carry

    lax.fori_loop(0, rounds, small, 0)

    def start_z(k, carry):
        z_copy(k).start()
        return carry

    lax.fori_loop(0, min(WINDOW, rounds), start_z, 0)

    def weight_grad(zblk, b):
        g = lax.dot_general(xv[b], zblk, (((0,), (0,)), ((), ())), preferred_element_type=F32)
        return g * (1.0 / tok)

    def add_terms(zblk, src, b):
        w = wfull[lax.div(src, halves), lax.rem(src, halves)].reshape(blk, blk)
        product = lax.dot_general(zblk, w, (((1,), (1,)), ((), ())), preferred_element_type=F32)
        part[...] = product.astype(BF16).reshape(part.shape)
        for s in range(slots):
            r = list_s[0, 0, s]
            m = lax.div(r, local_blocks)
            term = part[m].astype(F32)
            miss = jnp.full((blk, blk), r - m * local_blocks - b, jnp.int32)
            acc[s] = acc[s] + jnp.where(miss == 0, term, 0.0)

    def dp_copy(slot, j):
        return remote(sbuf.at[slot], sumr.at[d], dp_s.at[slot], dp_r.at[d], {"dp": j})

    def err_copy(j):
        return pltpu.make_async_copy(eout.at[j], err_o.at[0, 0, j], eo_s.at[j])

    def feedback(slot, j, grads):
        total = grads + errv[j]
        keep = jnp.full((blk, blk), mask_s[0, 0, j], jnp.int32) == 1
        eout[j] = jnp.where(keep, 0.0, total)
        err_copy(j).start()
        sent = jnp.where(keep, total, 0.0).astype(BF16)
        sbuf[slot] = sent

        @pl.when(j != d)
        def _():
            dp_copy(slot, j).start()

        @pl.when(j == d)
        def _():
            sumr[d] = sent

    for load in (*x_loads, err_load):
        load.wait()
    for s in range(slots):
        acc[s] = jnp.zeros((blk, blk), F32)
    feedback(rounds, t, weight_grad(z_block(t), lax.rem(rows_s[0, t], local_blocks)))

    def got_idx(k, carry):
        idx_copy(k).wait_recv()
        return carry

    lax.fori_loop(0, rounds, got_idx, 0)
    to_smem = pltpu.make_async_copy(idx_in, idx_s, misc.at[0])
    to_smem.start()

    def got_w(k, carry):
        w_copy(k).wait_recv()
        return carry

    lax.fori_loop(0, rounds, got_w, 0)
    own_w.wait()
    keep_w = pltpu.make_async_copy(wz.at[:, half], wfull.at[:, half, part_of], misc.at[1])
    keep_w.start()

    def share(i, carry):
        w_share(i).start()
        return carry

    lax.fori_loop(0, n_dp - 1, share, 0)
    to_smem.wait()
    keep_w.wait()

    def got_share(i, carry):
        w_share(i).wait_recv()
        return carry
        return carry

    def returned(k):
        g_copy(k).wait_recv()
        feedback(k, to_of(k), grecv[k].astype(F32))

    def one_round(k, carry):
        z_copy(k).wait_recv()

        @pl.when(k + WINDOW < rounds)
        def _():
            z_copy(k + WINDOW).start()

        zblk = zrecv[k]
        b = lax.rem(idx_s[k, 0, t], local_blocks)
        gsend[k] = weight_grad(zblk, b).astype(BF16)
        g_copy(k).start()

        @pl.when(k == 0)
        def _():
            lax.fori_loop(0, n_dp - 1, got_share, 0)

        add_terms(zblk, from_of(k), b)

        @pl.when(k >= LAG)
        def _():
            returned(k - LAG)

        return carry

    lax.fori_loop(0, rounds, one_round, 0)
    add_terms(z_block(t), t, lax.rem(rows_s[0, t], local_blocks))
    live = live_s[0, 0, 0]
    for s in range(slots):
        packed[s] = jnp.where(jnp.full((blk, blk), live, jnp.int32) > s, acc[s], 0.0).astype(BF16)
    over = remote(packed, recv_o.at[0, 0], pp_s.at[0], pp_r.at[0], {"pipe": 1 - p})
    over.start()
    for k in range(rounds - LAG, rounds):
        returned(k)

    def dp_in(i, total):
        src = lax.rem(d + i, n_dp)
        remote(sbuf.at[0], sumr.at[src], dp_s.at[0], dp_r.at[src], {"dp": src}).wait_recv()
        return total + sumr[src].astype(F32)

    sumv[...] = lax.fori_loop(1, n_dp, dp_in, sumr[d].astype(F32))
    out = pltpu.make_async_copy(sumv, sum_o.at[0, 0, 0], misc.at[2])
    out.start()

    def drain(k, carry):
        z_copy(k).wait_send()
        idx_copy(k).wait_send()
        w_copy(k).wait_send()
        g_copy(k).wait_send()
        err_copy(k).wait()

        @pl.when(to_of(k) != d)
        def _():
            dp_copy(k, to_of(k)).wait_send()

        return carry

    lax.fori_loop(0, rounds, drain, 0)
    err_copy(rounds).wait()

    @pl.when(t != d)
    def _():
        dp_copy(rounds, t).wait_send()

    def drain_share(i, carry):
        w_share(i).wait_send()
        return carry

    lax.fori_loop(0, n_dp - 1, drain_share, 0)
    over.wait()
    out.wait()


def local(n, n_dp, x_act, grad_z, weight_tiles, tile_rows, tile_cols, err_in, kept_mask, tile_list, live_count):
    tok, width = x_act.shape[1], x_act.shape[2]
    hidden = grad_z.shape[2]
    blk = weight_tiles.shape[2]
    slots = tile_list.shape[2]
    rounds = n - 1
    chunks = min(8, n_dp)
    rows = blk // chunks
    halves = n_dp // chunks
    dma = pltpu.SemaphoreType.DMA
    hbm = pl.BlockSpec(memory_space=pl.ANY)
    smem = pl.BlockSpec(memory_space=pltpu.SMEM)
    return pl.pallas_call(
        functools.partial(kernel, n, n_dp),
        out_shape=(
            jax.ShapeDtypeStruct((1, 1, slots, blk, blk), BF16),
            jax.ShapeDtypeStruct((1, 1, n, blk, blk), F32),
            jax.ShapeDtypeStruct((1, 1, 1, blk, blk), F32),
        ),
        in_specs=[hbm] * 4 + [smem] * 5,
        out_specs=(hbm, hbm, hbm),
        scratch_shapes=[
            pltpu.VMEM((width // blk, tok, blk), BF16),
            pltpu.VMEM((hidden // blk, tok, blk), BF16),
            pltpu.VMEM((n, blk, blk), F32),
            pltpu.VMEM((rounds, tok, blk), BF16),
            pltpu.VMEM((rounds, tok, blk), BF16),
            pltpu.VMEM((n // halves, halves, rows, blk), BF16),
            pltpu.VMEM((n // halves, halves, chunks, rows, blk), BF16),
            pltpu.VMEM((1, blk), jnp.int32),
            pltpu.VMEM((rounds, 1, blk), jnp.int32),
            pltpu.SMEM((rounds, 1, blk), jnp.int32),
            pltpu.VMEM((rounds, blk, blk), BF16),
            pltpu.VMEM((rounds, blk, blk), BF16),
            pltpu.VMEM((n, blk, blk), F32),
            pltpu.VMEM((n, blk, blk), BF16),
            pltpu.VMEM((n_dp, blk, blk), BF16),
            pltpu.VMEM((blk, blk), F32),
            pltpu.VMEM((tok // blk, blk, blk), BF16),
            pltpu.VMEM((slots, blk, blk), F32),
            pltpu.VMEM((slots, blk, blk), BF16),
            dma((hidden // blk,)), dma((width // blk,)), dma((2,)),
            dma((rounds,)), dma((rounds,)),
            dma((rounds,)), dma((rounds,)),
            dma((n_dp - 1,)), dma((n_dp - 1,)),
            dma((rounds,)), dma((rounds,)),
            dma((rounds,)), dma((rounds,)),
            dma((n,)), dma((n_dp,)),
            dma((1,)), dma((1,)),
            dma((n,)),
            dma((3,)),
        ],
        compiler_params=pltpu.CompilerParams(
            collective_id=0, has_side_effects=True, vmem_limit_bytes=40 * 2**20
        ),
        cost_estimate=pl.CostEstimate(flops=10**9, bytes_accessed=5 * 10**6, transcendentals=0),
    )(x_act, grad_z, weight_tiles, err_in, tile_rows, tile_cols, kept_mask, tile_list, live_count)


def solution(mesh):
    n, n_dp = mesh.shape["tensor"], mesh.shape["dp"]
    return jax.shard_map(
        functools.partial(local, n, n_dp),
        mesh=mesh,
        in_specs=(
            P("pipe", "dp", "tensor"),
            P("pipe", "dp", "tensor"),
            P("pipe", "tensor", None, None),
            P("pipe", "tensor"),
            P("pipe", "tensor"),
            P("pipe", "dp", "tensor", None, None),
            P("pipe", "dp", "tensor"),
            P("pipe", "dp", "tensor"),
            P("pipe", "dp", "tensor"),
        ),
        out_specs=(
            P("pipe", "dp", "tensor", None, None),
            P("pipe", "dp", "tensor", None, None),
            P("pipe", "dp", "tensor", None, None),
        ),
        check_vma=False,
    )
```

time: 351 us -> 135 us (0.38)
  the two profiles are of different devices: /device:TPU:32 before, /device:TPU:2 now
where the time goes in v1:
time: 135 us; the launch traced here: 134 us
  Pallas kernels  123 us (91%)
  local copies, waits for them, and re-layouts  9.66 us (7%)
    pallas_call x1, Pallas kernels, local(): pl.pallas_call(functools.partial(kernel, n, n_dp), out_shape=(jax.ShapeDt...  123 us
    unnamed x19, local copies, waits for them, and re-layouts  9.66 us

profile of v1, /device:TPU:2, one launch (start us, length us, event | category | flops | bytes accessed | tf_op | source)
XLA Modules:
  0.0 134.3 jit_solution(13645051456582361978)
XLA Ops:
  1.3 0.0 copy-start
  1.3 1.3 copy-done
  2.6 0.0 copy-start.1
  2.6 1.2 copy-done.1
  3.8 0.0 copy-start.2
  3.8 1.1 copy-done.2
  4.9 0.0 copy-start.3
  4.9 1.0 copy-done.3
  6.0 0.0 copy-start.4
  6.0 0.7 copy-done.4
  6.6 0.0 copy-start.5
  6.6 0.7 copy-done.5
  7.3 0.0 copy-start.6
  7.3 0.7 copy-done.6
  8.0 0.0 copy-start.7
  8.0 0.7 copy-done.7
  8.6 123.3 %shard_map.112 = (bf16[1,1,12,128,128]{4,3,2,1,0:T(8,128)(2,1)S(1)}, f32[1,1,16,128,128]{4,3,2,1,0:T(8,128)S(1)}, f32[1,1,1,128,128]{4,3,2,1,0:T(8,128)S(1)}) custom-call(bf16[1,384,1024]{2,1,0:T(8,128)(2,1)S(1)} %copy-done.2, bf16[1,384,1664]{2,1,0:T(8,128)(2,1)S(1)} %copy-done, bf16[1,16,128,128]{3,2,1,0:T(8,128)(2,1)S(1)} %copy-done.3, ...), custom_call_target="tpu_custom_call" | custom-call | flops 1000000000 | bytes 5000000 | tf_op jit(solution)/shard_map/pallas_call | solution.py:291
  131.9 0.7 copy.16
  132.7 1.0 copy.17
  133.7 0.6 copy.18
Async XLA Ops:
  1.3 1.3 copy-start
  2.6 1.2 copy-start.1
  3.8 1.1 copy-start.2
  4.9 1.0 copy-start.3
  6.0 0.7 copy-start.4
  6.6 0.7 copy-start.5
  7.3 0.7 copy-start.6
  8.0 0.7 copy-start.7

commit v2 on v1

--- a/solution.py
+++ b/solution.py
@@ -9,18 +9,20 @@
 
 MESH = pl.DeviceIdType.MESH
 WINDOW = 4
-LAG = 2
+LAG = 3
+TERM_LAG = 3
 BF16, F32 = jnp.bfloat16, jnp.float32
 
 
 def kernel(
-    n, n_dp, x_hbm, z_hbm, w_hbm, err_hbm, rows_s, cols_s, mask_s, list_s, live_s,
+    n, n_dp, x_hbm, z_hbm, w_hbm, err_hbm, cols_h, rows_h, mask_h, list_h, live_h,
     recv_o, err_o, sum_o,
-    xv, zv, errv, zsend, zrecv, wz, wfull, idx_out, idx_in, idx_s, gsend, grecv, eout, sbuf, sumr, sumv, part, acc, packed,
-    zl_sem, xl_sem, load_sem, ix_s, ix_r, ws_s, ws_r, wb_s, wb_r, zs_s, zs_r, gr_s, gr_r, dp_s, dp_r, pp_s, pp_r, eo_s, misc,
+    cols_s, rows_s, mask_s, list_s, live_s, xv, zv, errv, zsend, zrecv, wz, wfull, idx_out, idx_in, idx_s, gsend, grecv, eout, sbuf, sumr, sumv, part, acc, packed,
+    int_sem, zl_sem, xl_sem, load_sem, ix_s, ix_r, ws_s, ws_r, wb_s, wb_r, zs_s, zs_r, gr_s, gr_r, dp_s, dp_r, pp_s, pp_r, eo_s, misc,
 ):
     tok, blk = zsend.shape[1], zsend.shape[2]
     rounds = n - 1
+    term_lag = min(TERM_LAG, rounds - 1)
     local_blocks, hidden_blocks = xv.shape[0], zv.shape[0]
     slots = acc.shape[0]
     chunks, chunk_rows = wfull.shape[2], wfull.shape[3]
@@ -29,9 +31,12 @@
     halves = n_dp // chunks
 
     def offset(k):
-        q = k + 1
+        q = lax.rem(k + rounds - 2, rounds) + 1
         dist = n // 2 - lax.div(q, 2)
         return dist + (1 - lax.rem(q, 2)) * (n - 2 * dist)
+
+    def carries(rank):
+        return lax.rem(rank, halves) == half
 
     def to_of(k):
         return lax.rem(t + offset(k), n)
@@ -52,16 +57,38 @@
 
     def w_copy(k):
         src = w_hbm.at[0, to_of(k), pl.ds(pl.multiple_of(part_of * chunk_rows, chunk_rows), chunk_rows)]
-        return remote(src, wz.at[lax.div(t, halves), lax.rem(t, halves)], ws_s.at[k], ws_r.at[k], {"tensor": to_of(k)})
+        return remote(src, wz.at[lax.div(t, halves)], ws_s.at[k], ws_r.at[k], {"tensor": to_of(k)})
 
     def w_share(i):
         return remote(
-            wz.at[:, half], wfull.at[:, half, part_of], wb_s.at[i], wb_r.at[i], {"dp": lax.rem(d + i + 1, n_dp)}
+            wz, wfull.at[:, half, part_of], wb_s.at[i], wb_r.at[i], {"dp": lax.rem(d + i + 1, n_dp)}
         )
 
     def g_copy(k):
         return remote(gsend.at[k], grecv.at[k], gr_s.at[k], gr_r.at[k], {"tensor": from_of(k)})
 
+    barrier = pltpu.get_barrier_semaphore()
+
+    def greet_z(i, carry):
+        pl.semaphore_signal(barrier, inc=1, device_id={"tensor": lax.rem(t + i, n)}, device_id_type=MESH)
+        return carry
+
+    def greet_dp(i, carry):
+        pl.semaphore_signal(barrier, inc=1, device_id={"dp": lax.rem(d + i, n_dp)}, device_id_type=MESH)
+        return carry
+
+    lax.fori_loop(1, n, greet_z, 0)
+    lax.fori_loop(1, n_dp, greet_dp, 0)
+    pl.semaphore_signal(barrier, inc=1, device_id={"pipe": 1 - p}, device_id_type=MESH)
+
+    int_loads = [
+        pltpu.make_async_copy(src, dst, int_sem.at[i])
+        for i, (src, dst) in enumerate(
+            ((cols_h, cols_s), (rows_h, rows_s), (mask_h, mask_s), (list_h, list_s), (live_h, live_s))
+        )
+    ]
+    for load in int_loads:
+        load.start()
     z_loads = [
         pltpu.make_async_copy(z_hbm.at[0, :, pl.ds(i * blk, blk)], zv.at[i], zl_sem.at[i])
         for i in range(hidden_blocks)
@@ -71,29 +98,10 @@
         for i in range(local_blocks)
     ]
     err_load = pltpu.make_async_copy(err_hbm.at[0, 0], errv, load_sem.at[0])
-    for load in (*z_loads, *x_loads, err_load):
+    for load in z_loads:
         load.start()
-    own_w = pltpu.make_async_copy(
-        w_hbm.at[0, t, pl.ds(pl.multiple_of(part_of * chunk_rows, chunk_rows), chunk_rows)],
-        wz.at[lax.div(t, halves), lax.rem(t, halves)],
-        load_sem.at[1],
-    )
-    own_w.start()
-
-    barrier = pltpu.get_barrier_semaphore()
-
-    def greet_z(i, carry):
-        pl.semaphore_signal(barrier, inc=1, device_id={"tensor": lax.rem(t + i, n)}, device_id_type=MESH)
-        return carry
-
-    def greet_dp(i, carry):
-        pl.semaphore_signal(barrier, inc=1, device_id={"dp": lax.rem(d + i, n_dp)}, device_id_type=MESH)
-        return carry
-
-    lax.fori_loop(1, n, greet_z, 0)
-    lax.fori_loop(1, n_dp, greet_dp, 0)
-    pl.semaphore_signal(barrier, inc=1, device_id={"pipe": 1 - p}, device_id_type=MESH)
-
+    for load in int_loads:
+        load.wait()
     lane = lax.broadcasted_iota(jnp.int32, idx_out.shape, 1)
     row = jnp.zeros(idx_out.shape, jnp.int32)
     for j in range(n):
@@ -110,22 +118,38 @@
         zsend[k] = z_block(to_of(k))
         return carry
 
-    lax.fori_loop(0, rounds, pick, 0)
-
+    lax.fori_loop(0, min(WINDOW, rounds), pick, 0)
+
+    own_w = pltpu.make_async_copy(
+        w_hbm.at[0, t, pl.ds(pl.multiple_of(part_of * chunk_rows, chunk_rows), chunk_rows)],
+        wz.at[lax.div(t, halves)],
+        load_sem.at[1],
+    )
+
+    @pl.when(carries(t))
+    def _():
+        own_w.start()
+    for load in (*x_loads, err_load):
+        load.start()
     pl.semaphore_wait(barrier, n - 1 + n_dp - 1 + 1)
 
     def small(k, carry):
         idx_copy(k).start()
-        w_copy(k).start()
-        return carry
-
-    lax.fori_loop(0, rounds, small, 0)
+
+        @pl.when(carries(t))
+        def _():
+            w_copy(k).start()
+
+        return carry
+
 
     def start_z(k, carry):
         z_copy(k).start()
         return carry
 
+    lax.fori_loop(0, rounds, small, 0)
     lax.fori_loop(0, min(WINDOW, rounds), start_z, 0)
+    lax.fori_loop(min(WINDOW, rounds), rounds, pick, 0)
 
     def weight_grad(zblk, b):
         g = lax.dot_general(xv[b], zblk, (((0,), (0,)), ((), ())), preferred_element_type=F32)
@@ -179,12 +203,19 @@
     to_smem.start()
 
     def got_w(k, carry):
-        w_copy(k).wait_recv()
+        @pl.when(carries(from_of(k)))
+        def _():
+            w_copy(k).wait_recv()
+
         return carry
 
     lax.fori_loop(0, rounds, got_w, 0)
-    own_w.wait()
-    keep_w = pltpu.make_async_copy(wz.at[:, half], wfull.at[:, half, part_of], misc.at[1])
+
+    @pl.when(carries(t))
+    def _():
+        own_w.wait()
+
+    keep_w = pltpu.make_async_copy(wz, wfull.at[:, half, part_of], misc.at[1])
     keep_w.start()
 
     def share(i, carry):
@@ -204,6 +235,12 @@
         g_copy(k).wait_recv()
         feedback(k, to_of(k), grecv[k].astype(F32))
 
+    def local_of(k):
+        return lax.rem(idx_s[k, 0, t], local_blocks)
+
+    def terms(k):
+        add_terms(zrecv[k], from_of(k), local_of(k))
+
     def one_round(k, carry):
         z_copy(k).wait_recv()
 
@@ -211,16 +248,16 @@
         def _():
             z_copy(k + WINDOW).start()
 
-        zblk = zrecv[k]
-        b = lax.rem(idx_s[k, 0, t], local_blocks)
-        gsend[k] = weight_grad(zblk, b).astype(BF16)
+        gsend[k] = weight_grad(zrecv[k], local_of(k)).astype(BF16)
         g_copy(k).start()
 
-        @pl.when(k == 0)
+        @pl.when(k == term_lag)
         def _():
             lax.fori_loop(0, n_dp - 1, got_share, 0)
 
-        add_terms(zblk, from_of(k), b)
+        @pl.when(k >= term_lag)
+        def _():
+            terms(k - term_lag)
 
         @pl.when(k >= LAG)
         def _():
@@ -229,6 +266,7 @@
         return carry
 
     lax.fori_loop(0, rounds, one_round, 0)
+    lax.fori_loop(rounds - term_lag, rounds, lambda k, carry: (terms(k), carry)[1], 0)
     add_terms(z_block(t), t, lax.rem(rows_s[0, t], local_blocks))
     live = live_s[0, 0, 0]
     for s in range(slots):
@@ -238,6 +276,32 @@
     for k in range(rounds - LAG, rounds):
         returned(k)
 
+    def drain(k, carry):
+        z_copy(k).wait_send()
+        idx_copy(k).wait_send()
+        g_copy(k).wait_send()
+
+        @pl.when(carries(t))
+        def _():
+            w_copy(k).wait_send()
+
+        @pl.when(to_of(k) != d)
+        def _():
+            dp_copy(k, to_of(k)).wait_send()
+
+        return carry
+
+    def drain_share(i, carry):
+        w_share(i).wait_send()
+        return carry
+
+    lax.fori_loop(0, rounds, drain, 0)
+    lax.fori_loop(0, n_dp - 1, drain_share, 0)
+
+    @pl.when(t != d)
+    def _():
+        dp_copy(rounds, t).wait_send()
+
     def dp_in(i, total):
         src = lax.rem(d + i, n_dp)
         remote(sbuf.at[0], sumr.at[src], dp_s.at[0], dp_r.at[src], {"dp": src}).wait_recv()
@@ -247,33 +311,27 @@
     out = pltpu.make_async_copy(sumv, sum_o.at[0, 0, 0], misc.at[2])
     out.start()
 
-    def drain(k, carry):
-        z_copy(k).wait_send()
-        idx_copy(k).wait_send()
-        w_copy(k).wait_send()
-        g_copy(k).wait_send()
-        err_copy(k).wait()
-
-        @pl.when(to_of(k) != d)
-        def _():
-            dp_copy(k, to_of(k)).wait_send()
-
-        return carry
-
-    lax.fori_loop(0, rounds, drain, 0)
-    err_copy(rounds).wait()
-
-    @pl.when(t != d)
-    def _():
-        dp_copy(rounds, t).wait_send()
-
-    def drain_share(i, carry):
-        w_share(i).wait_send()
-        return carry
-
-    lax.fori_loop(0, n_dp - 1, drain_share, 0)
+    def drain_err(j, carry):
+        err_copy(j).wait()
+        return carry
+
+    lax.fori_loop(0, n, drain_err, 0)
     over.wait()
     out.wait()
+
+
+def hand_over(tiles_in, err_in, sum_in, tiles_out, err_out, sum_out, tiles, err, total, sem):
+    steps = [(tiles_in, tiles, tiles_out), (sum_in, total, sum_out)]
+    steps += [(err_in.at[0, 0, j], err.at[0, 0, j], err_out.at[0, 0, j]) for j in range(err_in.shape[2])]
+    arriving = [pltpu.make_async_copy(src, mid, sem.at[0, i]) for i, (src, mid, _) in enumerate(steps)]
+    leaving = [pltpu.make_async_copy(mid, dst, sem.at[1, i]) for i, (_, mid, dst) in enumerate(steps)]
+    for copy in arriving:
+        copy.start()
+    for before, after in zip(arriving, leaving):
+        before.wait()
+        after.start()
+    for copy in leaving:
+        copy.wait()
 
 
 def local(n, n_dp, x_act, grad_z, weight_tiles, tile_rows, tile_cols, err_in, kept_mask, tile_list, live_count):
@@ -287,23 +345,25 @@
     halves = n_dp // chunks
     dma = pltpu.SemaphoreType.DMA
     hbm = pl.BlockSpec(memory_space=pl.ANY)
-    smem = pl.BlockSpec(memory_space=pltpu.SMEM)
-    return pl.pallas_call(
+    ints = (tile_cols, tile_rows, kept_mask, tile_list, live_count)
+    shapes = (
+        jax.ShapeDtypeStruct((1, 1, slots, blk, blk), BF16),
+        jax.ShapeDtypeStruct((1, 1, n, blk, blk), F32),
+        jax.ShapeDtypeStruct((1, 1, 1, blk, blk), F32),
+    )
+    results = pl.pallas_call(
         functools.partial(kernel, n, n_dp),
-        out_shape=(
-            jax.ShapeDtypeStruct((1, 1, slots, blk, blk), BF16),
-            jax.ShapeDtypeStruct((1, 1, n, blk, blk), F32),
-            jax.ShapeDtypeStruct((1, 1, 1, blk, blk), F32),
-        ),
-        in_specs=[hbm] * 4 + [smem] * 5,
+        out_shape=shapes,
+        in_specs=[hbm] * 9,
         out_specs=(hbm, hbm, hbm),
-        scratch_shapes=[
+        scratch_shapes=[pltpu.SMEM(a.shape, a.dtype) for a in ints]
+        + [
             pltpu.VMEM((width // blk, tok, blk), BF16),
             pltpu.VMEM((hidden // blk, tok, blk), BF16),
             pltpu.VMEM((n, blk, blk), F32),
             pltpu.VMEM((rounds, tok, blk), BF16),
             pltpu.VMEM((rounds, tok, blk), BF16),
-            pltpu.VMEM((n // halves, halves, rows, blk), BF16),
+            pltpu.VMEM((n // halves, rows, blk), BF16),
             pltpu.VMEM((n // halves, halves, chunks, rows, blk), BF16),
             pltpu.VMEM((1, blk), jnp.int32),
             pltpu.VMEM((rounds, 1, blk), jnp.int32),
@@ -317,7 +377,7 @@
             pltpu.VMEM((tok // blk, blk, blk), BF16),
             pltpu.VMEM((slots, blk, blk), F32),
             pltpu.VMEM((slots, blk, blk), BF16),
-            dma((hidden // blk,)), dma((width // blk,)), dma((2,)),
+            dma((len(ints),)), dma((hidden // blk,)), dma((width // blk,)), dma((2,)),
             dma((rounds,)), dma((rounds,)),
             dma((rounds,)), dma((rounds,)),
             dma((n_dp - 1,)), dma((n_dp - 1,)),
@@ -329,10 +389,17 @@
             dma((3,)),
         ],
         compiler_params=pltpu.CompilerParams(
-            collective_id=0, has_side_effects=True, vmem_limit_bytes=40 * 2**20
+            collective_id=0, has_side_effects=True, vmem_limit_bytes=56 * 2**20
         ),
         cost_estimate=pl.CostEstimate(flops=10**9, bytes_accessed=5 * 10**6, transcendentals=0),
-    )(x_act, grad_z, weight_tiles, err_in, tile_rows, tile_cols, kept_mask, tile_list, live_count)
+    )(x_act, grad_z, weight_tiles, err_in, *ints)
+    return pl.pallas_call(
+        hand_over,
+        out_shape=shapes,
+        in_specs=[hbm] * 3,
+        out_specs=(hbm,) * 3,
+        scratch_shapes=[pltpu.VMEM(shape.shape, shape.dtype) for shape in shapes] + [dma((2, n + 2))],
+    )(*results)
 
 
 def solution(mesh):

time: 135 us -> 124 us (0.919)
  the two profiles are of different devices: /device:TPU:2 before, /device:TPU:38 now
where the time goes in v2:
time: 124 us
  Pallas kernels  123 us (99%)
  between operations  1.29 us (1%)
    pallas_call x1, Pallas kernels, local(): pl.pallas_call(functools.partial(kernel, n, n_dp), out_shape=shapes, in_s...  120 us

profile of v2, /device:TPU:38, one launch (start us, length us, event | category | flops | bytes accessed | tf_op | source)
XLA Modules:
  0.0 123.9 jit_solution(10598711290470917059)
XLA Ops:
  1.3 120.2 %shard_map.112 = (bf16[1,1,12,128,128]{4,3,2,1,0:T(8,128)(2,1)}, f32[1,1,16,128,128]{4,3,2,1,0:T(8,128)}, f32[1,1,1,128,128]{4,3,2,1,0:T(8,128)}) custom-call(bf16[1,384,1024]{2,1,0:T(8,128)(2,1)} %x_hbm.1, bf16[1,384,1664]{2,1,0:T(8,128)(2,1)} %z_hbm.1, bf16[1,16,128,128]{3,2,1,0:T(8,128)(2,1)} %w_hbm.1, f32[1,1,16,128,128]{4,3,2,1,0:T(8,128)} %err_hbm.1, ...), custom_call_target="tpu_custom_call" | custom-call | flops 1000000000 | bytes 5000000 | tf_op jit(solution)/shard_map/pallas_call | solution.py:354
  121.5 2.4 %shard_map.113 = (bf16[1,1,12,128,128]{4,3,2,1,0:T(8,128)(2,1)}, f32[1,1,16,128,128]{4,3,2,1,0:T(8,128)}, f32[1,1,1,128,128]{4,3,2,1,0:T(8,128)}) custom-call(bf16[1,1,12,128,128]{4,3,2,1,0:T(8,128)(2,1)} %get-tuple-element.6.tiles_in, f32[1,1,16,128,128]{4,3,2,1,0:T(8,128)} %get-tuple-element.7.err_in, f32[1,1,1,128,128]{4,3,2,1,0:T(8,128)} %get-tuple-element.8.sum_in), custom_call_target="tpu_custom_call" | custom-call | tf_op jit(solution)/shard_map/pallas_call | solution.py:396

commit v3 on v2

--- a/solution.py
+++ b/solution.py
@@ -322,7 +322,8 @@
 
 def hand_over(tiles_in, err_in, sum_in, tiles_out, err_out, sum_out, tiles, err, total, sem):
     steps = [(tiles_in, tiles, tiles_out), (sum_in, total, sum_out)]
-    steps += [(err_in.at[0, 0, j], err.at[0, 0, j], err_out.at[0, 0, j]) for j in range(err_in.shape[2])]
+    piece = err_in.shape[2] // 4
+    steps += [tuple(ref.at[0, 0, j * piece : j * piece + piece] for ref in (err_in, err, err_out)) for j in range(4)]
     arriving = [pltpu.make_async_copy(src, mid, sem.at[0, i]) for i, (src, mid, _) in enumerate(steps)]
     leaving = [pltpu.make_async_copy(mid, dst, sem.at[1, i]) for i, (_, mid, dst) in enumerate(steps)]
     for copy in arriving:
@@ -398,7 +399,7 @@
         out_shape=shapes,
         in_specs=[hbm] * 3,
         out_specs=(hbm,) * 3,
-        scratch_shapes=[pltpu.VMEM(shape.shape, shape.dtype) for shape in shapes] + [dma((2, n + 2))],
+        scratch_shapes=[pltpu.VMEM(shape.shape, shape.dtype) for shape in shapes] + [dma((2, 6))],
     )(*results)
 
 

time: 124 us -> 124 us (level)
  no operation moved by 1% of the time
where the time goes in v3:
time: 124 us
  Pallas kernels  122 us (98%)
  between operations  1.29 us (1%)
    pallas_call x1, Pallas kernels, local(): pl.pallas_call(functools.partial(kernel, n, n_dp), out_shape=shapes, in_s...  120 us

profile of v3, /device:TPU:38, one launch (start us, length us, event | category | flops | bytes accessed | tf_op | source)
XLA Modules:
  0.0 123.7 jit_solution(13151653222524201501)
XLA Ops:
  1.3 120.2 %shard_map.112 = (bf16[1,1,12,128,128]{4,3,2,1,0:T(8,128)(2,1)}, f32[1,1,16,128,128]{4,3,2,1,0:T(8,128)}, f32[1,1,1,128,128]{4,3,2,1,0:T(8,128)}) custom-call(bf16[1,384,1024]{2,1,0:T(8,128)(2,1)} %x_hbm.1, bf16[1,384,1664]{2,1,0:T(8,128)(2,1)} %z_hbm.1, bf16[1,16,128,128]{3,2,1,0:T(8,128)(2,1)} %w_hbm.1, f32[1,1,16,128,128]{4,3,2,1,0:T(8,128)} %err_hbm.1, ...), custom_call_target="tpu_custom_call" | custom-call | flops 1000000000 | bytes 5000000 | tf_op jit(solution)/shard_map/pallas_call | solution.py:355
  121.5 2.2 %shard_map.113 = (bf16[1,1,12,128,128]{4,3,2,1,0:T(8,128)(2,1)}, f32[1,1,16,128,128]{4,3,2,1,0:T(8,128)}, f32[1,1,1,128,128]{4,3,2,1,0:T(8,128)}) custom-call(bf16[1,1,12,128,128]{4,3,2,1,0:T(8,128)(2,1)} %get-tuple-element.6.tiles_in, f32[1,1,16,128,128]{4,3,2,1,0:T(8,128)} %get-tuple-element.7.err_in, f32[1,1,1,128,128]{4,3,2,1,0:T(8,128)} %get-tuple-element.8.sum_in), custom_call_target="tpu_custom_call" | custom-call | tf_op jit(solution)/shard_map/pallas_call | solution.py:397

commit v4 on v3

--- a/solution.py
+++ b/solution.py
@@ -251,56 +251,49 @@
         gsend[k] = weight_grad(zrecv[k], local_of(k)).astype(BF16)
         g_copy(k).start()
 
+        @pl.when(k >= LAG)
+        def _():
+            returned(k - LAG)
+
         @pl.when(k == term_lag)
         def _():
             lax.fori_loop(0, n_dp - 1, got_share, 0)
+            add_terms(z_block(t), t, lax.rem(rows_s[0, t], local_blocks))
 
         @pl.when(k >= term_lag)
         def _():
             terms(k - term_lag)
 
-        @pl.when(k >= LAG)
-        def _():
-            returned(k - LAG)
-
         return carry
 
     lax.fori_loop(0, rounds, one_round, 0)
+    def drain(k, carry):
+        z_copy(k).wait_send()
+        idx_copy(k).wait_send()
+        g_copy(k).wait_send()
+
+        @pl.when(carries(t))
+        def _():
+            w_copy(k).wait_send()
+
+        return carry
+
+    def drain_share(i, carry):
+        w_share(i).wait_send()
+        return carry
+
+    for k in range(rounds - LAG, rounds - 1):
+        returned(k)
     lax.fori_loop(rounds - term_lag, rounds, lambda k, carry: (terms(k), carry)[1], 0)
-    add_terms(z_block(t), t, lax.rem(rows_s[0, t], local_blocks))
     live = live_s[0, 0, 0]
     for s in range(slots):
         packed[s] = jnp.where(jnp.full((blk, blk), live, jnp.int32) > s, acc[s], 0.0).astype(BF16)
     over = remote(packed, recv_o.at[0, 0], pp_s.at[0], pp_r.at[0], {"pipe": 1 - p})
     over.start()
-    for k in range(rounds - LAG, rounds):
-        returned(k)
-
-    def drain(k, carry):
-        z_copy(k).wait_send()
-        idx_copy(k).wait_send()
-        g_copy(k).wait_send()
-
-        @pl.when(carries(t))
-        def _():
-            w_copy(k).wait_send()
-
-        @pl.when(to_of(k) != d)
-        def _():
-            dp_copy(k, to_of(k)).wait_send()
-
-        return carry
-
-    def drain_share(i, carry):
-        w_share(i).wait_send()
-        return carry
-
-    lax.fori_loop(0, rounds, drain, 0)
     lax.fori_loop(0, n_dp - 1, drain_share, 0)
-
-    @pl.when(t != d)
-    def _():
-        dp_copy(rounds, t).wait_send()
+    lax.fori_loop(0, rounds - 2, drain, 0)
+    returned(rounds - 1)
+    lax.fori_loop(rounds - 2, rounds, drain, 0)
 
     def dp_in(i, total):
         src = lax.rem(d + i, n_dp)
@@ -315,7 +308,20 @@
         err_copy(j).wait()
         return carry
 
+    def drain_dp(k, carry):
+        @pl.when(to_of(k) != d)
+        def _():
+            dp_copy(k, to_of(k)).wait_send()
+
+        return carry
+
     lax.fori_loop(0, n, drain_err, 0)
+    lax.fori_loop(0, rounds, drain_dp, 0)
+
+    @pl.when(t != d)
+    def _():
+        dp_copy(rounds, t).wait_send()
+
     over.wait()
     out.wait()
 

time: 124 us -> 125 us (level)
  no operation moved by 1% of the time
where the time goes in v4:
time: 125 us; the launch traced here: 124 us
  Pallas kernels  123 us (98%)
  between operations  1.29 us (1%)
    pallas_call x1, Pallas kernels, local(): pl.pallas_call(functools.partial(kernel, n, n_dp), out_shape=shapes, in_s...  121 us

profile of v4, /device:TPU:38, one launch (start us, length us, event | category | flops | bytes accessed | tf_op | source)
XLA Modules:
  0.0 124.4 jit_solution(16041907129111752152)
XLA Ops:
  1.3 120.9 %shard_map.112 = (bf16[1,1,12,128,128]{4,3,2,1,0:T(8,128)(2,1)}, f32[1,1,16,128,128]{4,3,2,1,0:T(8,128)}, f32[1,1,1,128,128]{4,3,2,1,0:T(8,128)}) custom-call(bf16[1,384,1024]{2,1,0:T(8,128)(2,1)} %x_hbm.1, bf16[1,384,1664]{2,1,0:T(8,128)(2,1)} %z_hbm.1, bf16[1,16,128,128]{3,2,1,0:T(8,128)(2,1)} %w_hbm.1, f32[1,1,16,128,128]{4,3,2,1,0:T(8,128)} %err_hbm.1, ...), custom_call_target="tpu_custom_call" | custom-call | flops 1000000000 | bytes 5000000 | tf_op jit(solution)/shard_map/pallas_call | solution.py:361
  122.2 2.2 %shard_map.113 = (bf16[1,1,12,128,128]{4,3,2,1,0:T(8,128)(2,1)}, f32[1,1,16,128,128]{4,3,2,1,0:T(8,128)}, f32[1,1,1,128,128]{4,3,2,1,0:T(8,128)}) custom-call(bf16[1,1,12,128,128]{4,3,2,1,0:T(8,128)(2,1)} %get-tuple-element.6.tiles_in, f32[1,1,16,128,128]{4,3,2,1,0:T(8,128)} %get-tuple-element.7.err_in, f32[1,1,1,128,128]{4,3,2,1,0:T(8,128)} %get-tuple-element.8.sum_in), custom_call_target="tpu_custom_call" | custom-call | tf_op jit(solution)/shard_map/pallas_call | solution.py:403
